TPU v7x, 512 devices: a whole 4x4x16 slice. The times are simulated.
512 devices in a mesh: tile: 32 (over x, z_hi, y), tag: 16 (over z_lo, core).
Axes of the slice: x: 4, y: 4, z: 16 (z_hi: 2, z_lo: 8; z = z_hi * 8 + z_lo), core: 2. Of those that a mesh axis runs over, the one named last changes fastest.
Arguments:
- tracers: float32 [96, 8, 8, 6144], P('tile', None, None, 'tag'), may hold values from 0.05 to 5
- eastward_mass: float32 [96, 8, 9, 64], P('tile', None, None, 'tag'), may hold values from -0.15 to 0.15
- eastward_courant: float32 [96, 8, 9, 64], P('tile', None, None, 'tag'), may hold values from -0.9 to 0.9
- northward_mass: float32 [96, 9, 8, 64], P('tile', None, None, 'tag'), may hold values from -0.15 to 0.15
- northward_courant: float32 [96, 9, 8, 64], P('tile', None, None, 'tag'), may hold values from -0.9 to 0.9
- thickness: float32 [96, 8, 8, 64], P('tile', None, None, 'tag'), may hold values from 1 to 2
- neighbor: int32 [96, 4], replicated, may hold values from 0 to 95, as said below
- orientation: int32 [96, 4], replicated, may hold values from 0 to 7, as said below
Outputs:
- tracers_next: float32 [96, 8, 8, 6144], P('tile', None, None, 'tag')
Inputs may be any that keep to these rules, and one draw needn't show every extreme that they name: The tiles are those of a cube surface of 6 faces of 4 x 4 tiles, numbered in an arbitrary order, each with its own right-handed cell frame in one of four quarter-turn orientations; neighbor and orientation describe which side of which tile meets each side, and the matching is symmetric. orientation[t, s] = 2 s' + f, with s' the side of tile neighbor[t, s] that meets side s of t, and f = 1 where the two tiles number the cells along that edge in opposite directions.
All inputs are finite; a program needn't handle non-finite values.
Results may differ from a plain program's by a relative error of at most 0.0003.
Values sent between devices are 32-bit elements; how exact they have to be, the bound alone decides.
A program may use at most 128 MiB of HBM per device.

v0:
```python
import jax
import jax.numpy as jnp
from jax import lax
from jax.sharding import PartitionSpec as P

LEV = 64


seven_twelfths = 7.0 / 12.0
one_twelfth = 1.0 / 12.0


def edge_strips(tile_cells):
    west_side = jnp.stack([tile_cells[:, :, 0], tile_cells[:, :, 1]], 1)
    east_side = jnp.stack([tile_cells[:, :, -1], tile_cells[:, :, -2]], 1)
    south_side = jnp.stack([tile_cells[:, 0], tile_cells[:, 1]], 1)
    north_side = jnp.stack([tile_cells[:, -1], tile_cells[:, -2]], 1)
    return jnp.stack([west_side, east_side, south_side, north_side], 1)


def face_flux(wide_cells, mass_face, courant_face, along_axis, edge_cells):
    outer_low = lax.slice_in_dim(wide_cells, 0, edge_cells + 1, axis=along_axis)
    inner_low = lax.slice_in_dim(wide_cells, 1, edge_cells + 2, axis=along_axis)
    inner_high = lax.slice_in_dim(wide_cells, 2, edge_cells + 3, axis=along_axis)
    outer_high = lax.slice_in_dim(wide_cells, 3, edge_cells + 4, axis=along_axis)
    mass_wide = mass_face[:, :, :, None, :]
    courant_wide = courant_face[:, :, :, None, :]
    face_value = seven_twelfths * (inner_low + inner_high) - one_twelfth * (outer_low + outer_high)
    return mass_wide * (face_value - 0.5 * courant_wide * (inner_high - inner_low))


def fetch_halo(tile_cells, my_partner, my_code):
    strips = edge_strips(tile_cells)
    shard_strips = lax.all_gather(strips, "tile", axis=0, tiled=True)
    shard_count = shard_strips.shape[0]
    inside = (my_partner >= 0) & (my_partner < shard_count)
    picked = shard_strips[jnp.clip(my_partner, 0, shard_count - 1), my_code // 2]
    turned = jnp.flip(picked, 3)
    chosen = jnp.where((my_code % 2 == 1)[:, :, None, None, None, None], turned, picked)
    return jnp.where(inside[:, :, None, None, None, None], chosen, 0.0)


def advance_tiles(
    tile_cells,
    my_partner,
    my_code,
    eastward_mass,
    eastward_courant,
    northward_mass,
    northward_courant,
    thickness,
):
    edge_cells = tile_cells.shape[1]
    halo_cells = fetch_halo(tile_cells, my_partner, my_code)
    west_cols = jnp.stack([halo_cells[:, 0, 1], halo_cells[:, 0, 0]], 2)
    east_cols = jnp.stack([halo_cells[:, 1, 0], halo_cells[:, 1, 1]], 2)
    south_rows = jnp.stack([halo_cells[:, 2, 1], halo_cells[:, 2, 0]], 1)
    north_rows = jnp.stack([halo_cells[:, 3, 0], halo_cells[:, 3, 1]], 1)
    wide_along = jnp.concatenate([west_cols, tile_cells, east_cols], 2)
    wide_across = jnp.concatenate([south_rows, tile_cells, north_rows], 1)
    flux_along = face_flux(wide_along, eastward_mass, eastward_courant, 2, edge_cells)
    flux_across = face_flux(wide_across, northward_mass, northward_courant, 1, edge_cells)
    divergence = (
        flux_along[:, :, 1:] - flux_along[:, :, :-1] + flux_across[:, 1:] - flux_across[:, :-1]
    )
    mass_change = (
        eastward_mass[:, :, 1:]
        - eastward_mass[:, :, :-1]
        + northward_mass[:, 1:]
        - northward_mass[:, :-1]
    )
    new_thickness = thickness - mass_change
    return (tile_cells * thickness[:, :, :, None, :] - divergence) / new_thickness[:, :, :, None, :]


def shards(
    tracers,
    eastward_mass,
    eastward_courant,
    northward_mass,
    northward_courant,
    thickness,
    neighbor,
    orientation,
):
    tile_count = tracers.shape[0]
    edge_cells = tracers.shape[1]
    tag_count = tracers.shape[3] // LEV
    first_tile = lax.axis_index("tile") * tile_count
    my_partner = lax.dynamic_slice_in_dim(neighbor, first_tile, tile_count, 0)
    my_code = lax.dynamic_slice_in_dim(orientation, first_tile, tile_count, 0)
    tag_major = tracers.reshape(tile_count, edge_cells, edge_cells, tag_count, LEV)
    full_east, full_east_courant, full_north, full_north_courant, full_thickness = (
        lax.all_gather(eastward_mass, "tag", axis=3, tiled=True),
        lax.all_gather(eastward_courant, "tag", axis=3, tiled=True),
        lax.all_gather(northward_mass, "tag", axis=3, tiled=True),
        lax.all_gather(northward_courant, "tag", axis=3, tiled=True),
        lax.all_gather(thickness, "tag", axis=3, tiled=True),
    )
    stepped = advance_tiles(
        tag_major,
        my_partner,
        my_code,
        full_east,
        full_east_courant,
        full_north,
        full_north_courant,
        full_thickness,
    )
    return stepped.reshape(tile_count, edge_cells, edge_cells, tag_count * LEV)


def solution(mesh):
    return jax.shard_map(
        shards,
        mesh=mesh,
        in_specs=(
            P("tile", None, None, "tag"),
            P("tile", None, None, "tag"),
            P("tile", None, None, "tag"),
            P("tile", None, None, "tag"),
            P("tile", None, None, "tag"),
            P("tile", None, None, "tag"),
            P(),
            P(),
        ),
        out_specs=P("tile", None, None, "tag"),
        check_vma=False,
    )
```

profile of v0, /device:TPU:1, one launch (start us, length us, event | category | flops | bytes accessed | tf_op | source)
XLA Modules:
  0.0 649.7 jit_solution(13348266925586438005)
XLA Ops:
  6.5 0.0 copy-start
  6.5 0.0 copy-start.1
  6.5 0.0 all-gather.2.cloned.1.call-start
  6.5 1.1 reshape.16
  7.9 1.1 pad_maximum_fusion.12
  8.9 0.0 all-gather.2.cloned.1.call-update
  9.0 0.8 fusion.19
  9.7 0.1 copy.98
  9.8 0.1 reshape.18
  9.9 0.8 copy.92
  10.7 48.5 %all_gather.19 = f32[3,8,9,64]{2,1,0,3:T(8,128)S(1)} all-gather(f32[3,8,9,4]{2,1,0,3:T(8,128)S(1)} %copy.92), channel_id=1, replica_groups=mesh['tile'=32,'tag'=16] {'tag'}, dimensions={3}, use_global_device_ids=true | all-gather | bytes 58752 | tf_op jit(solution)/shard_map/all_gather | solution.py:94
  59.2 0.3 copy.93
  59.6 0.8 copy.107
  60.4 33.0 %all_gather.21 = f32[3,8,9,64]{2,1,0,3:T(8,128)S(1)} all-gather(f32[3,8,9,4]{2,1,0,3:T(8,128)S(1)} %copy.107), channel_id=1, replica_groups=mesh['tile'=32,'tag'=16] {'tag'}, dimensions={3}, use_global_device_ids=true | all-gather | bytes 58752 | tf_op jit(solution)/shard_map/all_gather | solution.py:95
  93.4 0.3 copy.108
  93.7 0.8 copy.110
  94.6 59.5 %all_gather.22 = f32[3,9,8,64]{1,2,0,3:T(8,128)S(1)} all-gather(f32[3,9,8,4]{1,2,0,3:T(8,128)S(1)} %copy.110), channel_id=1, replica_groups=mesh['tile'=32,'tag'=16] {'tag'}, dimensions={3}, use_global_device_ids=true | all-gather | bytes 58752 | tf_op jit(solution)/shard_map/all_gather | solution.py:96
  154.1 1.0 copy.111
  155.0 0.8 copy.118
  155.8 67.5 %all_gather.23 = f32[3,9,8,64]{1,2,0,3:T(8,128)S(1)} all-gather(f32[3,9,8,4]{1,2,0,3:T(8,128)S(1)} %copy.118), channel_id=1, replica_groups=mesh['tile'=32,'tag'=16] {'tag'}, dimensions={3}, use_global_device_ids=true | all-gather | bytes 58752 | tf_op jit(solution)/shard_map/all_gather | solution.py:97
  223.3 1.0 copy.119
  224.3 1.2 fusion.23
  225.4 1.4 copy.129
  226.8 1.2 copy.130
  228.0 0.8 copy.90
  228.8 62.4 %all_gather.18 = f32[3,8,8,64]{2,1,0,3:T(8,128)S(1)} all-gather(f32[3,8,8,4]{2,1,0,3:T(8,128)S(1)} %copy.90), channel_id=1, replica_groups=mesh['tile'=32,'tag'=16] {'tag'}, dimensions={3}, use_global_device_ids=true | all-gather | bytes 52224 | tf_op jit(solution)/shard_map/all_gather | solution.py:98
  291.2 0.9 copy.91
  292.1 2.3 fusion.13
  294.4 1.4 copy.122
  295.8 0.0 copy-done
  295.8 0.0 copy-done.1
  295.8 0.1 fusion.16
  295.9 0.9 broadcast_multiply_fusion
  296.8 333.1 %all-gather.2.cloned.1.call-done = f32[96,4,2,8,6,64]{5,4,3,2,0,1:T(8,128)} async-done(((f32[3,4,2,8,6,64]{5,4,3,2,0,1:T(8,128)}), f32[96,4,2,8,6,64]{5,4,3,2,0,1:T(8,128)}) %all-gather.2.cloned.1.call-update) | async-done | bytes 9437200 | tf_op jit(solution)/shard_map/all_gather | solution.py:34
  630.0 8.8 %gather_fusion = f32[12,2,8,6,64]{4,3,2,1,0:T(8,128)S(1)} fusion(f32[96,4,2,8,6,64]{5,4,3,2,0,1:T(8,128)} %all-gather.2.cloned.1.call-done, s32[12]{0:T(128)S(1)} %reshape.18), kind=kCustom, calls=%fused_computation | custom fusion | bytes 589920 | tf_op jit(solution)/shard_map/gather | solution.py:37
  638.7 0.1 copy.100
  638.8 0.2 fusion.10
  639.0 0.1 slice_bitcast_fusion.6
  639.0 0.5 fusion.9
  639.5 1.2 fusion.4
  640.8 1.2 fusion.15
  642.0 0.9 reshape.17
  (6 shorter events, 0.2 us)
Async XLA Ops:
  6.5 289.3 %copy-start = (s32[96,4]{0,1:T(4,128)S(1)}, s32[96,4]{0,1:T(4,128)}, u32[]{:S(2)}) copy-start(s32[96,4]{0,1:T(4,128)} %param.14) | copy-start | bytes 4612
  6.5 289.3 %copy-start.1 = (s32[96,4]{0,1:T(4,128)S(1)}, s32[96,4]{0,1:T(4,128)}, u32[]{:S(2)}) copy-start(s32[96,4]{0,1:T(4,128)} %param.15) | copy-start | bytes 4612
  6.5 623.4 %all-gather.2.cloned.1.call-start = ((), (), s32[]{:S(2)}) async-start(), calls=%async_computation | async-start | bytes 25952256 | tf_op jit(solution)/shard_map/all_gather | solution.py:34
Sparse Core Ops, SparseCore 0:
  11.7 618.2 all-gather.1
where the time goes:
time: 650 us
  waiting for transfers between devices  333 us (51%)
  blocking collectives  271 us (42%)
  local copies, waits for them, and re-layouts  23.7 us (4%)
  between operations  13.5 us (2%)
  other arithmetic  8.35 us (1%)
    all_gather x1, waiting for transfers between devices, fetch_halo(): shard_strips = lax.all_gather(strips, 'tile', axis=0, tiled=True)  333 us
    all_gather x1, blocking collectives, shards(): lax.all_gather(northward_courant, 'tag', axis=3, tiled=True)  67.5 us
    all_gather x1, blocking collectives, shards(): lax.all_gather(thickness, 'tag', axis=3, tiled=True)  62.4 us
    all_gather x1, blocking collectives, shards(): lax.all_gather(northward_mass, 'tag', axis=3, tiled=True)  59.5 us
    all_gather x1, blocking collectives, shards(): lax.all_gather(eastward_mass, 'tag', axis=3, tiled=True)  48.5 us
    all_gather x1, blocking collectives, shards(): lax.all_gather(eastward_courant, 'tag', axis=3, tiled=True)  33 us
  transfers between devices with their start and end apart: 1, of which 1 were waited for; matrix products, arithmetic and copies ran while one was open for 3% of the time, Pallas kernels for 0%

commit v1 on v0

v1 whole, which is shorter than its diff:
```python
import jax
import jax.numpy as jnp
from jax import lax
from jax.experimental import pallas as pl
from jax.experimental.pallas import tpu as pltpu
from jax.sharding import PartitionSpec as P

MESH = pl.DeviceIdType.MESH
T = 3
C = 8
K = 16
Z = 8
CH = 3
ROWS = 9
SIDES = 12
FW = 384


def collector_cells(k):
    cy, cx, dy, dx = k // 8, k // 4 % 2, k // 2 % 2, k % 2
    far = lambda flag, d: 7 - d if flag else d
    corner = (far(cy, dy), far(cx, dx))
    across_x = (5 - dy if cy else 2 + dy, far(1 - cx, dx))
    across_y = (far(1 - cy, dy), 5 - dx if cx else 2 + dx)
    return corner, across_x, across_y


def kernel(q, mx, cx_ref, my, cy_ref, th, nbr, ori, out, s1, r1a, r1b, r1c, s2, r2a, r2b, r2c, halo, flow, wide, grid,
           acc, kx, ky, pick, place, ready, ssem1, rsem1, ssem2, rsem2, fright, fleft, fsend, fcore, fcsend):
    r1, r2 = (r1a, r1b, r1c), (r2a, r2b, r2c)
    tile, tag = lax.axis_index("tile"), lax.axis_index("tag")
    x, half, y = tile // 8, lax.rem(tile // 4, 2), lax.rem(tile, 4)
    me = x * 4 + y
    z, core = tag // 2, lax.rem(tag, 2)
    cy, cx = me // 8, lax.rem(me // 4, 2)

    def member(k, h):
        return ((k // 4) * 8 + h * 4 + lax.rem(k, 4), tag)

    def line(zz):
        return (tile, zz * 2 + core)

    twin = (tile, z * 2 + 1 - core)
    barrier = pltpu.get_barrier_semaphore()

    def greet(dev):
        pl.semaphore_signal(barrier, inc=1, device_id=dev, device_id_type=MESH)

    def greet_plane(i, carry):
        greet(member(lax.rem(me + i, K), half))
        return carry

    lax.fori_loop(1, K, greet_plane, 0)
    greet(twin)

    @pl.when(z > 0)
    def _():
        greet(line(z - 1))

    @pl.when(z < Z - 1)
    def _():
        greet(line(z + 1))

    def all_rows(ref, sem, rows):
        pltpu.make_async_copy(ref.at[pl.ds(0, rows)], ref.at[pl.ds(0, rows)], sem).wait()

    def stage(t, carry):
        for k in range(K):
            for slot, (j, i) in enumerate(collector_cells(k)):
                for c in range(CH):
                    s1[c, k, t * 3 + slot] = q[t, j, i:i + 1, c * 128:(c + 1) * 128]
        return carry

    lax.fori_loop(0, T, stage, 0)

    near = K + jnp.where(z > 0, 1, 0) + jnp.where(z < Z - 1, 1, 0)

    @pl.when(half == 0)
    def _():
        pl.semaphore_wait(barrier, near)

        def greet_far(i, carry):
            greet(member(lax.rem(me + i, K), 1))
            return carry

        lax.fori_loop(0, K, greet_far, 0)

    def first_copy(c, k, h):
        return pltpu.make_async_remote_copy(
            src_ref=s1.at[c, k], dst_ref=r1[c].at[pl.ds(tile * ROWS, ROWS)], send_sem=ssem1.at[c],
            recv_sem=rsem1.at[c], device_id=member(k, h), device_id_type=MESH)

    def send_far():
        for c in range(CH):
            def go(i, carry, c=c):
                first_copy(c, lax.rem(me + i, K), 1 - half).start()
                return carry

            lax.fori_loop(0, K, go, 0)

    @pl.when(half == 1)
    def _():
        pl.semaphore_wait(barrier, near + K)

        def answer(i, carry):
            pl.semaphore_signal(ready, inc=1, device_id=member(lax.rem(me + i, K), 0), device_id_type=MESH)
            return carry

        lax.fori_loop(0, K, answer, 0)
        send_far()

    for c in range(CH):
        def go(i, carry, c=c):
            first_copy(c, lax.rem(me + i, K), half).start()
            return carry

        lax.fori_loop(1, K, go, 0)
        r1[c][pl.ds(tile * ROWS, ROWS)] = s1[c, me]

    def pack(t, carry):
        flow[tag, t] = jnp.zeros((4, FW), jnp.float32)
        for j in range(C):
            for n, ref in enumerate((mx, cx_ref, my, cy_ref)):
                at = n * 72 + j * 9
                flow[tag, t, :, at:at + 9] = ref[t, j]
            at = 288 + j * 8
            flow[tag, t, :, at:at + 8] = th[t, j]
        return carry

    lax.fori_loop(0, T, pack, 0)

    def block(zz):
        return flow.at[zz * 2 + core]

    def pass_on(zz, dev, sem, done):
        return pltpu.make_async_remote_copy(src_ref=block(zz), dst_ref=block(zz), send_sem=done, recv_sem=sem,
                                            device_id=dev, device_id_type=MESH)

    for s in range(Z):
        for way, step, sems, here, inner in ((0, -1, fright, z >= s, z < Z - 1), (1, 1, fleft, z + s < Z, z > 0)):
            zz = z + step * s
            if s == 0 and step == -1:
                pass_on(z, twin, fcore, fcsend).start()
            if s:
                @pl.when(here)
                def _():
                    pass_on(zz, twin, sems.at[s - 1], fcsend).wait_recv()
                    pass_on(zz, twin, fcore, fcsend).start()

            if s < Z - 1:
                @pl.when(here & inner)
                def _():
                    pass_on(zz, line(z - step), sems.at[s], fsend.at[way, s]).start()

    @pl.when(half == 0)
    def _():
        pl.semaphore_wait(ready, K)
        send_far()

    def find(n, carry):
        k, r = n // SIDES, lax.rem(n, SIDES)
        t, s = r // 4, lax.rem(r, 4)
        home = ((k // 4) * 8 + half * 4 + lax.rem(k, 4)) * T + t
        side = ori[s, home] // 2
        b = lax.rem(side, 2)
        slot = jnp.where(side // 2 == 1, jnp.where(b == cy, 0, 2), jnp.where(b == cx, 0, 1))
        pick[n] = nbr[s, home] * 3 + slot
        return carry

    lax.fori_loop(0, K * SIDES, find, 0)

    def locate(r, carry):
        t, s = r // 4, lax.rem(r, 4)
        code = ori[s, tile * T + t]
        flip, b, is_y = lax.rem(code, 2), lax.rem(code // 2, 2), code // 4
        for d in range(2):
            for a in range(C):
                a2, a1, a0 = a // 4, a // 2 % 2, a % 2
                end = 1 - flip if a2 else flip
                cross = 1 - b if a1 != a2 else b
                deep = a0 ^ a2
                kx_at = end * 8 + cross * 4 + deep * 2 + d
                ky_at = cross * 8 + end * 4 + d * 2 + deep
                place[r * 16 + d * 8 + a] = jnp.where(is_y == 1, ky_at, kx_at) * SIDES + r
        return carry

    lax.fori_loop(0, SIDES, locate, 0)

    all_rows(flow, fcore, Z)

    def turn(t, carry):
        for g in range(2 * Z):
            wide[4 * g:4 * g + 4, :] = flow[g, t]
            wide[64 + 4 * g:68 + 4 * g, :] = flow[g, t]
        for p in range(FW // 128):
            grid[t, p * 128:(p + 1) * 128, :] = wide[:, p * 128:(p + 1) * 128].T
        return carry

    lax.fori_loop(0, T, turn, 0)

    row = lax.broadcasted_iota(jnp.int32, (C, 128), 0)

    def stencil(m_low, c_low, m_high, c_high, scale):
        m_low, m_high = m_low * scale, m_high * scale
        low, high = m_low * (1.0 / 12.0), m_high * (1.0 / 12.0)
        return (
            -low,
            m_low * (7.0 / 12.0 + 0.5 * c_low) + high,
            m_low * (7.0 / 12.0 - 0.5 * c_low) - m_high * (7.0 / 12.0 + 0.5 * c_high),
            -m_high * (7.0 / 12.0 - 0.5 * c_high) - low,
            high,
        )

    def inner_step(t, carry):
        for j in range(C):
            x_low, x_high = grid[t, 9 * j:9 * j + 8, :], grid[t, 9 * j + 1:9 * j + 9, :]
            xc_low, xc_high = grid[t, 72 + 9 * j:80 + 9 * j, :], grid[t, 73 + 9 * j:81 + 9 * j, :]
            y_low, y_high = grid[t, pl.ds(144 + j, 8, stride=9), :], grid[t, pl.ds(145 + j, 8, stride=9), :]
            yc_low, yc_high = grid[t, pl.ds(216 + j, 8, stride=9), :], grid[t, pl.ds(217 + j, 8, stride=9), :]
            thick = grid[t, 288 + 8 * j:296 + 8 * j, :]
            scale = 1.0 / (thick - (x_high - x_low + y_high - y_low))
            xs = stencil(x_low, xc_low, x_high, xc_high, scale)
            ys = stencil(y_low, yc_low, y_high, yc_high, scale)
            centre = thick * scale + xs[2] + ys[2]
            for n, (v, i) in enumerate(((xs[1], 0), (xs[0], 0), (xs[0], 1), (xs[3], 7), (xs[4], 7), (xs[4], 6))):
                kx[t, n, j:j + 1, :] = v[i:i + 1, :]
            for n, (v, at) in enumerate(((ys[1], 0), (ys[0], 0), (ys[0], 1), (ys[3], 7), (ys[4], 7), (ys[4], 6))):
                if at == j:
                    ky[t, n] = v
            xm2 = jnp.where(row >= 2, xs[0], 0.0)
            xm1 = jnp.where(row >= 1, xs[1], 0.0)
            xp1 = jnp.where(row <= 6, xs[3], 0.0)
            xp2 = jnp.where(row <= 5, xs[4], 0.0)
            for c in range(CH):
                lanes = slice(c * 128, (c + 1) * 128)
                v = q[t, j, :, lanes]
                total = centre * v
                total += xm2 * pltpu.roll(v, 2, 0) + xm1 * pltpu.roll(v, 1, 0)
                total += xp1 * pltpu.roll(v, 7, 0) + xp2 * pltpu.roll(v, 6, 0)
                for step, w in ((-2, ys[0]), (-1, ys[1]), (1, ys[3]), (2, ys[4])):
                    if 0 <= j + step < C:
                        total += w * q[t, j + step, :, lanes]
                acc[c, t, 8 * j:8 * j + 8, :] = total
        return carry

    lax.fori_loop(0, T, inner_step, 0)

    def second_copy(c, k):
        return pltpu.make_async_remote_copy(
            src_ref=s2.at[c, k], dst_ref=r2[c].at[pl.ds(me * SIDES, SIDES)], send_sem=ssem2.at[c],
            recv_sem=rsem2.at[c], device_id=member(k, half), device_id_type=MESH)

    def collect(c):
        all_rows(r1[c], rsem1.at[c], (2 * K - 1) * ROWS)

        def choose(k, carry):
            for r in range(SIDES):
                s2[c, k, r] = r1[c][pick[k * SIDES + r]]
            return carry

        lax.fori_loop(0, K, choose, 0)

        def go(i, carry):
            second_copy(c, lax.rem(me + i, K)).start()
            return carry

        lax.fori_loop(1, K, go, 0)
        r2[c][pl.ds(me * SIDES, SIDES)] = s2[c, me]

    def finish(c):
        all_rows(r2[c], rsem2.at[c], (K - 1) * SIDES)

        def lay(r, carry):
            for d in range(2):
                for a in range(C):
                    halo[r, d, a:a + 1, :] = r2[c][place[r * 16 + d * 8 + a]]
            return carry

        lax.fori_loop(0, SIDES, lay, 0)

        def add(t, carry):
            west, east, south, north = ((halo[t * 4 + s, 0], halo[t * 4 + s, 1]) for s in range(4))
            for (one, two), n, edge, inside in ((west, 0, 0, 1), (east, 3, 7, 6)):
                acc[c, t, pl.ds(edge, 8, stride=8), :] += kx[t, n] * one + kx[t, n + 1] * two
                acc[c, t, pl.ds(inside, 8, stride=8), :] += kx[t, n + 2] * one
            for (one, two), n, edge, inside in ((south, 0, 0, 1), (north, 3, 7, 6)):
                acc[c, t, 8 * edge:8 * edge + 8, :] += ky[t, n] * one + ky[t, n + 1] * two
                acc[c, t, 8 * inside:8 * inside + 8, :] += ky[t, n + 2] * one
            for j in range(C):
                out[t, j, :, c * 128:(c + 1) * 128] = acc[c, t, 8 * j:8 * j + 8, :]
            return carry

        lax.fori_loop(0, T, add, 0)

    for c in range(CH):
        collect(c)
        if c:
            finish(c - 1)
    finish(CH - 1)

    for c in range(CH):
        all_rows(r1[c], ssem1.at[c], (2 * K - 1) * ROWS)
        all_rows(r2[c], ssem2.at[c], (K - 1) * SIDES)
    all_rows(flow, fcsend, Z)
    for s in range(Z - 1):
        for way, here in ((0, (z >= s) & (z < Z - 1)), (1, (z + s < Z) & (z > 0))):
            @pl.when(here)
            def _():
                pass_on(z, twin, fcore, fsend.at[way, s]).wait_send()


def shards(tracers, eastward_mass, eastward_courant, northward_mass, northward_courant, thickness, neighbor, orientation):
    f32 = jnp.float32
    vmem, smem = pl.BlockSpec(memory_space=pltpu.VMEM), pl.BlockSpec(memory_space=pltpu.SMEM)
    dma = pltpu.SemaphoreType.DMA
    return pl.pallas_call(
        kernel,
        out_shape=jax.ShapeDtypeStruct(tracers.shape, f32),
        in_specs=[vmem] * 6 + [smem] * 2,
        out_specs=vmem,
        scratch_shapes=[
            pltpu.VMEM((CH, K, ROWS, 1, 128), f32),
            *[pltpu.VMEM((2 * K * ROWS, 1, 128), f32)] * CH,
            pltpu.VMEM((CH, K, SIDES, 1, 128), f32),
            *[pltpu.VMEM((K * SIDES, 1, 128), f32)] * CH,
            pltpu.VMEM((SIDES, 2, C, 128), f32),
            pltpu.VMEM((2 * Z, T, 4, FW), f32),
            pltpu.VMEM((128, FW), f32),
            pltpu.VMEM((T, FW, 128), f32),
            pltpu.VMEM((CH, T, C * C, 128), f32),
            pltpu.VMEM((T, 6, C, 128), f32),
            pltpu.VMEM((T, 6, C, 128), f32),
            pltpu.SMEM((K * SIDES,), jnp.int32),
            pltpu.SMEM((SIDES * 16,), jnp.int32),
            pltpu.SemaphoreType.REGULAR,
            dma((CH,)), dma((CH,)), dma((CH,)), dma((CH,)),
            dma((Z,)), dma((Z,)), dma((2, Z)), dma, dma,
        ],
        compiler_params=pltpu.CompilerParams(collective_id=0, has_side_effects=True, vmem_limit_bytes=32 * 2**20),
    )(
        tracers,
        eastward_mass.transpose(0, 1, 3, 2),
        eastward_courant.transpose(0, 1, 3, 2),
        northward_mass.transpose(0, 2, 3, 1),
        northward_courant.transpose(0, 2, 3, 1),
        thickness.transpose(0, 1, 3, 2),
        neighbor.T,
        orientation.T,
    )


def solution(mesh):
    split = P("tile", None, None, "tag")
    return jax.shard_map(
        shards,
        mesh=mesh,
        in_specs=(split,) * 6 + (P(), P()),
        out_specs=split,
        check_vma=False,
    )
```

time: 650 us -> 81.8 us (0.13)
  the two profiles are of different devices: /device:TPU:1 before, /device:TPU:8 now
where the time goes in v1:
time: 81.8 us; the launch traced here: 81.3 us
  Pallas kernels  74.9 us (92%)
  local copies, waits for them, and re-layouts  6.36 us (8%)
    pallas_call x1, Pallas kernels, shards(): pl.pallas_call(kernel, out_shape=jax.ShapeDtypeStruct(tracers.shape, f32)...  74.9 us
    unnamed x17, local copies, waits for them, and re-layouts  6.36 us

profile of v1, /device:TPU:8, one launch (start us, length us, event | category | flops | bytes accessed | tf_op | source)
XLA Modules:
  0.0 81.3 jit_solution(8546223572707197877)
XLA Ops:
  0.0 0.0 copy-start.7
  0.0 0.0 copy-start.6
  0.0 0.7 copy-done.7
  0.7 0.0 copy-done.6
  0.7 0.0 copy-start
  0.7 1.0 %copy-done = f32[3,8,8,384]{3,2,1,0:T(8,128)S(1)} copy-done((f32[3,8,8,384]{3,2,1,0:T(8,128)S(1)}, f32[3,8,8,384]{3,2,1,0:T(8,128)}, u32[]{:S(2)}) %copy-start) | copy-done | bytes 294936
  1.7 0.0 copy-start.1
  1.7 0.8 copy-done.1
  2.5 0.0 copy-start.2
  2.5 0.8 copy-done.2
  3.3 0.0 copy-start.3
  3.3 0.8 copy-done.3
  4.1 0.0 copy-start.4
  4.1 0.8 copy-done.4
  4.9 0.0 copy-start.5
  4.9 0.8 copy-done.5
  5.7 74.9 %shard_map.82 = f32[3,8,8,384]{3,2,1,0:T(8,128)S(1)} custom-call(f32[3,8,8,384]{3,2,1,0:T(8,128)S(1)} %copy-done, f32[3,8,4,9]{3,2,1,0:T(4,128)S(1)} %bitcast.7, f32[3,8,4,9]{3,2,1,0:T(4,128)S(1)} %bitcast.8, f32[3,8,4,9]{3,2,1,0:T(4,128)S(1)} %bitcast.9, f32[3,8,4,9]{3,2,1,0:T(4,128)S(1)} %bitcast.10, f32[3,8,4,8]{3,2,1,0:T(4,128)S(1)} %bitcast.11, ...), custom_call_target="tpu_custom_call" | custom-call | tf_op jit(solution)/shard_map/pallas_call | solution.py:316
  80.6 0.7 copy.10
Async XLA Ops:
  0.0 0.7 copy-start.7
  0.0 0.7 copy-start.6
  0.7 1.0 %copy-start = (f32[3,8,8,384]{3,2,1,0:T(8,128)S(1)}, f32[3,8,8,384]{3,2,1,0:T(8,128)}, u32[]{:S(2)}) copy-start(f32[3,8,8,384]{3,2,1,0:T(8,128)} %q.1) | copy-start | bytes 884740
  1.7 0.8 copy-start.1
  2.5 0.8 copy-start.2
  3.3 0.8 copy-start.3
  4.1 0.8 copy-start.4
  4.9 0.8 copy-start.5

commit v2 on v1

v2 whole, which is shorter than its diff:
```python
import jax
import jax.numpy as jnp
from jax import lax
from jax.experimental import pallas as pl
from jax.experimental.pallas import tpu as pltpu
from jax.sharding import PartitionSpec as P

MESH = pl.DeviceIdType.MESH
T = 3
C = 8
REACH = 4
K = 16
Z = 8
CH = 3
ROWS = 9
SIDES = 12
FW = 384


def collector_cells(k):
    cy, cx, dy, dx = k // 8, k // 4 % 2, k // 2 % 2, k % 2
    far = lambda flag, d: 7 - d if flag else d
    corner = (far(cy, dy), far(cx, dx))
    across_x = (5 - dy if cy else 2 + dy, far(1 - cx, dx))
    across_y = (far(1 - cy, dy), 5 - dx if cx else 2 + dx)
    return corner, across_x, across_y


def kernel(q_in, mx_in, cx_in, my_in, cy_in, th_in, nbr_in, ori_in, out, q, mx, cx_ref, my, cy_ref, th, nbr, ori, load, s1, r1a, r1b, r1c, s2, r2a, r2b, r2c, halo, flow, wide, grid,
           acc, kx, ky, pick_v, place_v, pick, place, ready, ssem1, rsem1, ssem2, rsem2, fnear, fsend, fcore, fcsend):
    r1, r2 = (r1a, r1b, r1c), (r2a, r2b, r2c)
    tile, tag = lax.axis_index("tile"), lax.axis_index("tag")
    x, half, y = tile // 8, lax.rem(tile // 4, 2), lax.rem(tile, 4)
    me = x * 4 + y
    z, core = tag // 2, lax.rem(tag, 2)
    cy, cx = me // 8, lax.rem(me // 4, 2)

    def line(zz):
        return (tile, zz * 2 + core)

    inputs = [
        pltpu.make_async_copy(src, dst, load.at[n]) for n, (src, dst) in enumerate((
            (q_in, q), (mx_in, mx), (cx_in, cx_ref), (my_in, my), (cy_in, cy_ref), (th_in, th), (nbr_in, nbr), (ori_in, ori)))]
    for copy in inputs:
        copy.start()

    twin = (tile, z * 2 + 1 - core)
    barrier = pltpu.get_barrier_semaphore()

    def greet(dev):
        pl.semaphore_signal(barrier, inc=1, device_id=dev, device_id_type=MESH)

    xs = [jnp.where(x + i < 4, x + i, x + i - 4) for i in range(4)]
    ys = [jnp.where(y + i < 4, y + i, y + i - 4) for i in range(4)]
    ring = [(xs[i // 4] * 4 + ys[i % 4], xs[i // 4] * 8 + ys[i % 4]) for i in range(K)]

    def device(i, h):
        return (ring[i][1] + h * 4, tag)

    for i in range(1, K):
        greet(device(i, half))
    greet(twin)

    @pl.when(half == 0)
    def _():
        for i in range(K):
            greet(device(i, 1))

    def on_line(zz):
        return (zz >= 0) & (zz < Z)

    for d in range(1, REACH + 1):
        for way in (-1, 1):
            @pl.when(on_line(z + way * d))
            def _():
                greet(line(z + way * d))

    near = K + jnp.minimum(z, REACH) + jnp.minimum(Z - 1 - z, REACH)

    def all_rows(ref, sem, rows):
        pltpu.make_async_copy(ref.at[pl.ds(0, rows)], ref.at[pl.ds(0, rows)], sem).wait()

    inputs[6].wait()
    inputs[7].wait()
    code = ori[...]
    flip, b, is_y = code & 1, (code >> 1) & 1, code >> 2 == 1
    slot = jnp.where(is_y, jnp.where(b == cy, 0, 2), jnp.where(b == cx, 0, 1))
    pick_v[...] = nbr[...] * 3 + slot
    side_row = lax.broadcasted_iota(jnp.int32, (4, 32 * T), 0)
    for d in range(2):
        for a in range(C):
            a2, a1, a0 = a // 4, a // 2 % 2, a % 2
            end = 1 - flip if a2 else flip
            cross = 1 - b if a1 != a2 else b
            deep = a0 ^ a2
            kx_at = end * 8 + cross * 4 + deep * 2 + d
            ky_at = cross * 8 + end * 4 + d * 2 + deep
            place_v[d * 8 + a] = jnp.where(is_y, ky_at, kx_at) * SIDES + side_row
    tables = [pltpu.make_async_copy(pick_v, pick, load.at[8]), pltpu.make_async_copy(place_v, place, load.at[9])]
    for copy in tables:
        copy.start()

    def stage(t, carry):
        for k in range(K):
            for slot, (j, i) in enumerate(collector_cells(k)):
                for c in range(CH):
                    s1[c, k, t * 3 + slot] = q[t, j, i:i + 1, c * 128:(c + 1) * 128]
        return carry

    inputs[0].wait()
    lax.fori_loop(0, T, stage, 0)

    def first_copy(c, i, h):
        return pltpu.make_async_remote_copy(
            src_ref=s1.at[c, ring[i][0]], dst_ref=r1[c].at[pl.ds(tile * ROWS, ROWS)], send_sem=ssem1.at[c],
            recv_sem=rsem1.at[c], device_id=device(i, h), device_id_type=MESH)

    def send_far():
        for c in range(CH):
            for i in range(K):
                first_copy(c, i, 1 - half).start()

    def pack(t, carry):
        flow[tag, t] = jnp.zeros((4, FW), jnp.float32)
        for j in range(C):
            for n, ref in enumerate((mx, cx_ref, my, cy_ref)):
                at = n * 72 + j * 9
                flow[tag, t, :, at:at + 9] = ref[t, j]
            at = 288 + j * 8
            flow[tag, t, :, at:at + 8] = th[t, j]
        return carry

    for copy in inputs[1:6]:
        copy.wait()
    lax.fori_loop(0, T, pack, 0)

    def block(zz):
        return flow.at[zz * 2 + core]

    def pass_on(zz, dev, sem, done):
        return pltpu.make_async_remote_copy(src_ref=block(zz), dst_ref=block(zz), send_sem=done, recv_sem=sem,
                                            device_id=dev, device_id_type=MESH)

    def flow_out():
        pass_on(z, twin, fcore, fcsend).start()
        for d in range(1, REACH + 1):
            for n, way in enumerate((-1, 1)):
                @pl.when(on_line(z + way * d))
                def _():
                    pass_on(z, line(z + way * d), fnear.at[1 - n, d], fsend.at[n, d]).start()

    def plane_out():
        for c in range(CH):
            for i in range(1, K):
                first_copy(c, i, half).start()
            r1[c][pl.ds(tile * ROWS, ROWS)] = s1[c, me]

    @pl.when(half == 0)
    def _():
        pl.semaphore_wait(barrier, near)
        flow_out()

    @pl.when(half == 1)
    def _():
        pl.semaphore_wait(barrier, near + K)
        for i in range(K):
            pl.semaphore_signal(ready, inc=1, device_id=device(i, 0), device_id_type=MESH)
        send_far()
        flow_out()

    plane_out()
    for d in (4, 1, 2, 3, 5, 6, 7):
        for n, way in enumerate((-1, 1)):
            @pl.when(on_line(z + way * d))
            def _():
                pass_on(z + way * d, twin, fnear.at[n, d], fcsend).wait_recv()
                pass_on(z + way * d, twin, fcore, fcsend).start()
                if d == REACH:
                    for e in range(1, Z - REACH):
                        @pl.when(on_line(z - way * e))
                        def _():
                            pass_on(z + way * d, line(z - way * e), fnear.at[n, d + e], fsend.at[n, d + e]).start()

    @pl.when(half == 0)
    def _():
        pl.semaphore_wait(ready, K)
        send_far()


    all_rows(flow, fcore, Z)

    def turn(t, carry):
        for g in range(2 * Z):
            wide[4 * g:4 * g + 4, :] = flow[g, t]
            wide[64 + 4 * g:68 + 4 * g, :] = flow[g, t]
        for p in range(FW // 128):
            grid[t, p * 128:(p + 1) * 128, :] = wide[:, p * 128:(p + 1) * 128].T
        return carry

    lax.fori_loop(0, T, turn, 0)

    row = lax.broadcasted_iota(jnp.int32, (C, 128), 0)

    def stencil(m_low, c_low, m_high, c_high, scale):
        m_low, m_high = m_low * scale, m_high * scale
        low, high = m_low * (1.0 / 12.0), m_high * (1.0 / 12.0)
        return (
            -low,
            m_low * (7.0 / 12.0 + 0.5 * c_low) + high,
            m_low * (7.0 / 12.0 - 0.5 * c_low) - m_high * (7.0 / 12.0 + 0.5 * c_high),
            -m_high * (7.0 / 12.0 - 0.5 * c_high) - low,
            high,
        )

    def inner_step(t, carry):
        for j in range(C):
            x_low, x_high = grid[t, 9 * j:9 * j + 8, :], grid[t, 9 * j + 1:9 * j + 9, :]
            xc_low, xc_high = grid[t, 72 + 9 * j:80 + 9 * j, :], grid[t, 73 + 9 * j:81 + 9 * j, :]
            y_low, y_high = grid[t, pl.ds(144 + j, 8, stride=9), :], grid[t, pl.ds(145 + j, 8, stride=9), :]
            yc_low, yc_high = grid[t, pl.ds(216 + j, 8, stride=9), :], grid[t, pl.ds(217 + j, 8, stride=9), :]
            thick = grid[t, 288 + 8 * j:296 + 8 * j, :]
            scale = 1.0 / (thick - (x_high - x_low + y_high - y_low))
            xs = stencil(x_low, xc_low, x_high, xc_high, scale)
            ys = stencil(y_low, yc_low, y_high, yc_high, scale)
            centre = thick * scale + xs[2] + ys[2]
            for n, (v, i) in enumerate(((xs[1], 0), (xs[0], 0), (xs[0], 1), (xs[3], 7), (xs[4], 7), (xs[4], 6))):
                kx[t, n, j:j + 1, :] = v[i:i + 1, :]
            for n, (v, at) in enumerate(((ys[1], 0), (ys[0], 0), (ys[0], 1), (ys[3], 7), (ys[4], 7), (ys[4], 6))):
                if at == j:
                    ky[t, n] = v
            xm2 = jnp.where(row >= 2, xs[0], 0.0)
            xm1 = jnp.where(row >= 1, xs[1], 0.0)
            xp1 = jnp.where(row <= 6, xs[3], 0.0)
            xp2 = jnp.where(row <= 5, xs[4], 0.0)
            for c in range(CH):
                lanes = slice(c * 128, (c + 1) * 128)
                v = q[t, j, :, lanes]
                total = centre * v
                total += xm2 * pltpu.roll(v, 2, 0) + xm1 * pltpu.roll(v, 1, 0)
                total += xp1 * pltpu.roll(v, 7, 0) + xp2 * pltpu.roll(v, 6, 0)
                for step, w in ((-2, ys[0]), (-1, ys[1]), (1, ys[3]), (2, ys[4])):
                    if 0 <= j + step < C:
                        total += w * q[t, j + step, :, lanes]
                acc[c, t, 8 * j:8 * j + 8, :] = total
        return carry

    lax.fori_loop(0, T, inner_step, 0)

    def second_copy(c, i):
        return pltpu.make_async_remote_copy(
            src_ref=s2.at[c, ring[i][0]], dst_ref=r2[c].at[pl.ds(me * SIDES, SIDES)], send_sem=ssem2.at[c],
            recv_sem=rsem2.at[c], device_id=device(i, half), device_id_type=MESH)

    for copy in tables:
        copy.wait()

    def collect(c):
        all_rows(r1[c], rsem1.at[c], (2 * K - 1) * ROWS)

        def choose(k, carry):
            home = ((k // 4) * 8 + half * 4 + lax.rem(k, 4)) * T
            for r in range(SIDES):
                s2[c, k, r] = r1[c][pick[r % 4, home + r // 4]]
            return carry

        lax.fori_loop(0, K, choose, 0)

        for i in range(1, K):
            second_copy(c, i).start()
        r2[c][pl.ds(me * SIDES, SIDES)] = s2[c, me]

    def finish(c):
        all_rows(r2[c], rsem2.at[c], (K - 1) * SIDES)

        def lay(t, carry):
            for s in range(4):
                for d in range(2):
                    for a in range(C):
                        halo[t * 4 + s, d, a:a + 1, :] = r2[c][place[d * 8 + a, s, tile * T + t] + 4 * t]
            return carry

        lax.fori_loop(0, T, lay, 0)

        def add(t, carry):
            west, east, south, north = ((halo[t * 4 + s, 0], halo[t * 4 + s, 1]) for s in range(4))
            for (one, two), n, edge, inside in ((west, 0, 0, 1), (east, 3, 7, 6)):
                acc[c, t, pl.ds(edge, 8, stride=8), :] += kx[t, n] * one + kx[t, n + 1] * two
                acc[c, t, pl.ds(inside, 8, stride=8), :] += kx[t, n + 2] * one
            for (one, two), n, edge, inside in ((south, 0, 0, 1), (north, 3, 7, 6)):
                acc[c, t, 8 * edge:8 * edge + 8, :] += ky[t, n] * one + ky[t, n + 1] * two
                acc[c, t, 8 * inside:8 * inside + 8, :] += ky[t, n + 2] * one
            for j in range(C):
                out[t, j, :, c * 128:(c + 1) * 128] = acc[c, t, 8 * j:8 * j + 8, :]
            return carry

        lax.fori_loop(0, T, add, 0)

    for c in range(CH):
        collect(c)
        if c:
            finish(c - 1)
    finish(CH - 1)

    for c in range(CH):
        all_rows(r1[c], ssem1.at[c], (2 * K - 1) * ROWS)
        all_rows(r2[c], ssem2.at[c], (K - 1) * SIDES)
    all_rows(flow, fcsend, Z)
    for n, way in enumerate((-1, 1)):
        for d in range(1, REACH + 1):
            @pl.when(on_line(z + way * d))
            def _():
                pass_on(z, twin, fcore, fsend.at[n, d]).wait_send()

        for e in range(1, Z - REACH):
            @pl.when(on_line(z + way * REACH) & on_line(z - way * e))
            def _():
                pass_on(z, twin, fcore, fsend.at[n, REACH + e]).wait_send()


def shards(tracers, eastward_mass, eastward_courant, northward_mass, northward_courant, thickness, neighbor, orientation):
    f32 = jnp.float32
    vmem, hbm = pl.BlockSpec(memory_space=pltpu.VMEM), pl.BlockSpec(memory_space=pltpu.HBM)
    dma = pltpu.SemaphoreType.DMA
    return pl.pallas_call(
        kernel,
        out_shape=pltpu.VMEM(tracers.shape, f32),
        in_specs=[hbm] * 8,
        out_specs=vmem,
        scratch_shapes=[
            pltpu.VMEM((T, C, C, 384), f32),
            *[pltpu.VMEM((T, C, 4, C + 1), f32)] * 4,
            pltpu.VMEM((T, C, 4, C), f32),
            *[pltpu.VMEM((4, 32 * T), jnp.int32)] * 2,
            dma((10,)),
            pltpu.VMEM((CH, K, ROWS, 1, 128), f32),
            *[pltpu.VMEM((2 * K * ROWS, 1, 128), f32)] * CH,
            pltpu.VMEM((CH, K, SIDES, 1, 128), f32),
            *[pltpu.VMEM((K * SIDES, 1, 128), f32)] * CH,
            pltpu.VMEM((SIDES, 2, C, 128), f32),
            pltpu.VMEM((2 * Z, T, 4, FW), f32),
            pltpu.VMEM((128, FW), f32),
            pltpu.VMEM((T, FW, 128), f32),
            pltpu.VMEM((CH, T, C * C, 128), f32),
            pltpu.VMEM((T, 6, C, 128), f32),
            pltpu.VMEM((T, 6, C, 128), f32),
            pltpu.VMEM((4, 32 * T), jnp.int32),
            pltpu.VMEM((16, 4, 32 * T), jnp.int32),
            pltpu.SMEM((4, 32 * T), jnp.int32),
            pltpu.SMEM((16, 4, 32 * T), jnp.int32),
            pltpu.SemaphoreType.REGULAR,
            dma((CH,)), dma((CH,)), dma((CH,)), dma((CH,)),
            dma((2, Z)), dma((2, Z)), dma, dma,
        ],
        compiler_params=pltpu.CompilerParams(collective_id=0, has_side_effects=True, vmem_limit_bytes=32 * 2**20),
    )(*(pltpu.with_memory_space_constraint(a, pltpu.HBM) for a in (
        tracers,
        eastward_mass.transpose(0, 1, 3, 2),
        eastward_courant.transpose(0, 1, 3, 2),
        northward_mass.transpose(0, 2, 3, 1),
        northward_courant.transpose(0, 2, 3, 1),
        thickness.transpose(0, 1, 3, 2),
        neighbor.T,
        orientation.T,
    )))


def solution(mesh):
    split = P("tile", None, None, "tag")
    return jax.shard_map(
        shards,
        mesh=mesh,
        in_specs=(split,) * 6 + (P(), P()),
        out_specs=split,
        check_vma=False,
    )
```

time: 81.8 us -> 49.9 us (0.61)
  the two profiles are of different devices: /device:TPU:8 before, /device:TPU:448 now
where the time goes in v2:
time: 49.9 us; the launch traced here: 49.8 us
  Pallas kernels  49.1 us (98%)
  local copies, waits for them, and re-layouts  0.72 us (1%)
    pallas_call x1, Pallas kernels, shards(): pl.pallas_call(kernel, out_shape=pltpu.VMEM(tracers.shape, f32), in_specs...  49.1 us

profile of v2, /device:TPU:448, one launch (start us, length us, event | category | flops | bytes accessed | tf_op | source)
XLA Modules:
  0.0 49.8 jit_solution(8339301199602661096)
XLA Ops:
  0.0 49.1 %shard_map.82 = f32[3,8,8,384]{3,2,1,0:T(8,128)S(1)} custom-call(f32[3,8,8,384]{3,2,1,0:T(8,128)} %q_in.1, f32[3,8,4,9]{3,2,1,0:T(4,128)} %bitcast.7, f32[3,8,4,9]{3,2,1,0:T(4,128)} %bitcast.8, f32[3,8,4,9]{3,2,1,0:T(4,128)} %bitcast.9, f32[3,8,4,9]{3,2,1,0:T(4,128)} %bitcast.10, f32[3,8,4,8]{3,2,1,0:T(4,128)} %bitcast.11, s32[4,96]{1,0:T(4,128)} %bitcast.12, ...), custom_call_target="tpu_custom_call" | custom-call | tf_op jit(solution)/shard_map/pallas_call | solution.py:324
  49.1 0.7 %copy.10 = f32[3,8,8,384]{3,2,1,0:T(8,128)} copy(f32[3,8,8,384]{3,2,1,0:T(8,128)S(1)} %shard_map.82) | data formatting | bytes 589824

commit v3 on v2

--- a/solution.py
+++ b/solution.py
@@ -8,6 +8,9 @@
 MESH = pl.DeviceIdType.MESH
 T = 3
 C = 8
+GROUPS = ((0, 1), (2,))
+PARTS = tuple((n, c) for n, g in enumerate(GROUPS) for c in g)
+EARLY = 4
 REACH = 4
 K = 16
 Z = 8
@@ -26,9 +29,9 @@
     return corner, across_x, across_y
 
 
-def kernel(q_in, mx_in, cx_in, my_in, cy_in, th_in, nbr_in, ori_in, out, q, mx, cx_ref, my, cy_ref, th, nbr, ori, load, s1, r1a, r1b, r1c, s2, r2a, r2b, r2c, halo, flow, wide, grid,
-           acc, kx, ky, pick_v, place_v, pick, place, ready, ssem1, rsem1, ssem2, rsem2, fnear, fsend, fcore, fcsend):
-    r1, r2 = (r1a, r1b, r1c), (r2a, r2b, r2c)
+def kernel(q_in, mx_in, cx_in, my_in, cy_in, th_in, nbr_in, ori_in, out, q, mx, cx_ref, my, cy_ref, th, nbr, ori, load, s1, r1a, r1b, s2, r2a, r2b, halo, flow, wide, grid,
+           acc, kx, ky, pick_v, place_v, pick, place, ready, ssem1, rsem1, sfar, rfar, ssem2, rsem2, fnear, fsend, fcore, fcsend):
+    r1, r2 = (r1a, r1b), (r2a, r2b)
     tile, tag = lax.axis_index("tile"), lax.axis_index("tag")
     x, half, y = tile // 8, lax.rem(tile // 4, 2), lax.rem(tile, 4)
     me = x * 4 + y
@@ -61,10 +64,16 @@
         greet(device(i, half))
     greet(twin)
 
+    early = z < EARLY
+
     @pl.when(half == 0)
     def _():
-        for i in range(K):
-            greet(device(i, 1))
+        greet(device(0, 1))
+
+        @pl.when(early)
+        def _():
+            for i in range(1, K):
+                greet(device(i, 1))
 
     def on_line(zz):
         return (zz >= 0) & (zz < Z)
@@ -80,45 +89,77 @@
     def all_rows(ref, sem, rows):
         pltpu.make_async_copy(ref.at[pl.ds(0, rows)], ref.at[pl.ds(0, rows)], sem).wait()
 
-    inputs[6].wait()
-    inputs[7].wait()
-    code = ori[...]
-    flip, b, is_y = code & 1, (code >> 1) & 1, code >> 2 == 1
-    slot = jnp.where(is_y, jnp.where(b == cy, 0, 2), jnp.where(b == cx, 0, 1))
-    pick_v[...] = nbr[...] * 3 + slot
-    side_row = lax.broadcasted_iota(jnp.int32, (4, 32 * T), 0)
-    for d in range(2):
-        for a in range(C):
-            a2, a1, a0 = a // 4, a // 2 % 2, a % 2
-            end = 1 - flip if a2 else flip
-            cross = 1 - b if a1 != a2 else b
-            deep = a0 ^ a2
-            kx_at = end * 8 + cross * 4 + deep * 2 + d
-            ky_at = cross * 8 + end * 4 + d * 2 + deep
-            place_v[d * 8 + a] = jnp.where(is_y, ky_at, kx_at) * SIDES + side_row
-    tables = [pltpu.make_async_copy(pick_v, pick, load.at[8]), pltpu.make_async_copy(place_v, place, load.at[9])]
-    for copy in tables:
-        copy.start()
-
     def stage(t, carry):
         for k in range(K):
             for slot, (j, i) in enumerate(collector_cells(k)):
                 for c in range(CH):
-                    s1[c, k, t * 3 + slot] = q[t, j, i:i + 1, c * 128:(c + 1) * 128]
+                    s1[k, c, t * 3 + slot] = q[t, j, i:i + 1, c * 128:(c + 1) * 128]
         return carry
 
     inputs[0].wait()
     lax.fori_loop(0, T, stage, 0)
 
-    def first_copy(c, i, h):
+    def first_copy(n, i):
         return pltpu.make_async_remote_copy(
-            src_ref=s1.at[c, ring[i][0]], dst_ref=r1[c].at[pl.ds(tile * ROWS, ROWS)], send_sem=ssem1.at[c],
-            recv_sem=rsem1.at[c], device_id=device(i, h), device_id_type=MESH)
+            src_ref=s1.at[ring[i][0], pl.ds(GROUPS[n][0], len(GROUPS[n]))], dst_ref=r1[n].at[me], send_sem=ssem1.at[n],
+            recv_sem=rsem1.at[n], device_id=device(i, half), device_id_type=MESH)
+
+    def far_copy(n, c):
+        at = c - GROUPS[n][0]
+        return pltpu.make_async_remote_copy(
+            src_ref=r1[n].at[pl.ds(0, K), at], dst_ref=r1[n].at[pl.ds(K, K), at], send_sem=sfar.at[c],
+            recv_sem=rfar.at[c], device_id=device(0, 1 - half), device_id_type=MESH)
+
+    def early_copy(n, c, i):
+        return pltpu.make_async_remote_copy(
+            src_ref=s1.at[ring[i][0], c], dst_ref=r1[n].at[K + me, c - GROUPS[n][0]], send_sem=sfar.at[c], recv_sem=rfar.at[c],
+            device_id=device(i, 0), device_id_type=MESH)
 
     def send_far():
-        for c in range(CH):
-            for i in range(K):
-                first_copy(c, i, 1 - half).start()
+        for n in range(len(GROUPS)):
+            all_rows(r1[n], rsem1.at[n], K - 1)
+
+        @pl.when((half == 0) | jnp.logical_not(early))
+        def _():
+            for n, c in PARTS:
+                far_copy(n, c).start()
+
+    def block(zz):
+        return flow.at[zz * 2 + core]
+
+    def pass_on(zz, dev, sem, done):
+        return pltpu.make_async_remote_copy(src_ref=block(zz), dst_ref=block(zz), send_sem=done, recv_sem=sem,
+                                            device_id=dev, device_id_type=MESH)
+
+    def flow_out():
+        pass_on(z, twin, fcore, fcsend).start()
+        for d in range(1, REACH + 1):
+            for n, way in enumerate((-1, 1)):
+                @pl.when(on_line(z + way * d))
+                def _():
+                    pass_on(z, line(z + way * d), fnear.at[1 - n, d], fsend.at[n, d]).start()
+
+    def plane_out():
+        for n in range(len(GROUPS)):
+            for i in range(1, K):
+                first_copy(n, i).start()
+        for n, c in PARTS:
+            r1[n][me, c - GROUPS[n][0]] = s1[me, c]
+
+    @pl.when(half == 0)
+    def _():
+        pl.semaphore_wait(barrier, near)
+
+    @pl.when(half == 1)
+    def _():
+        pl.semaphore_wait(barrier, near + jnp.where(early, K, 1))
+        pl.semaphore_signal(ready, inc=1, device_id=device(0, 0), device_id_type=MESH)
+
+        @pl.when(early)
+        def _():
+            for n, c in PARTS:
+                for i in range(K):
+                    early_copy(n, c, i).start()
 
     def pack(t, carry):
         flow[tag, t] = jnp.zeros((4, FW), jnp.float32)
@@ -134,41 +175,34 @@
         copy.wait()
     lax.fori_loop(0, T, pack, 0)
 
-    def block(zz):
-        return flow.at[zz * 2 + core]
-
-    def pass_on(zz, dev, sem, done):
-        return pltpu.make_async_remote_copy(src_ref=block(zz), dst_ref=block(zz), send_sem=done, recv_sem=sem,
-                                            device_id=dev, device_id_type=MESH)
-
-    def flow_out():
-        pass_on(z, twin, fcore, fcsend).start()
-        for d in range(1, REACH + 1):
-            for n, way in enumerate((-1, 1)):
-                @pl.when(on_line(z + way * d))
-                def _():
-                    pass_on(z, line(z + way * d), fnear.at[1 - n, d], fsend.at[n, d]).start()
-
-    def plane_out():
-        for c in range(CH):
-            for i in range(1, K):
-                first_copy(c, i, half).start()
-            r1[c][pl.ds(tile * ROWS, ROWS)] = s1[c, me]
-
-    @pl.when(half == 0)
-    def _():
-        pl.semaphore_wait(barrier, near)
-        flow_out()
+    flow_out()
+    plane_out()
+
+    inputs[6].wait()
+    inputs[7].wait()
+    code = ori[...]
+    flip, b, is_y = code & 1, (code >> 1) & 1, code >> 2 == 1
+    slot = jnp.where(is_y, jnp.where(b == cy, 0, 2), jnp.where(b == cx, 0, 1))
+    home = (nbr[...] * 171) >> 9
+    away = jnp.where(((home >> 2) & 1) == half, 0, K)
+    pick_v[...] = (away + (home >> 3) * 4 + (home & 3)) * 16 + (nbr[...] - 3 * home) * 3 + slot
+    for d in range(2):
+        for a in range(C):
+            a2, a1, a0 = a // 4, a // 2 % 2, a % 2
+            end = 1 - flip if a2 else flip
+            cross = 1 - b if a1 != a2 else b
+            deep = a0 ^ a2
+            kx_at = end * 8 + cross * 4 + deep * 2 + d
+            ky_at = cross * 8 + end * 4 + d * 2 + deep
+            place_v[d * 8 + a] = jnp.where(is_y, ky_at, kx_at)
+    tables = [pltpu.make_async_copy(pick_v, pick, load.at[8]), pltpu.make_async_copy(place_v, place, load.at[9])]
+    for copy in tables:
+        copy.start()
 
     @pl.when(half == 1)
     def _():
-        pl.semaphore_wait(barrier, near + K)
-        for i in range(K):
-            pl.semaphore_signal(ready, inc=1, device_id=device(i, 0), device_id_type=MESH)
         send_far()
-        flow_out()
-
-    plane_out()
+
     for d in (4, 1, 2, 3, 5, 6, 7):
         for n, way in enumerate((-1, 1)):
             @pl.when(on_line(z + way * d))
@@ -181,11 +215,10 @@
                         def _():
                             pass_on(z + way * d, line(z - way * e), fnear.at[n, d + e], fsend.at[n, d + e]).start()
 
-    @pl.when(half == 0)
-    def _():
-        pl.semaphore_wait(ready, K)
+    @pl.when((half == 0) & jnp.logical_not(((z != 2) & (z != 1))))
+    def _():
+        pl.semaphore_wait(ready, 1)
         send_far()
-
 
     all_rows(flow, fcore, Z)
 
@@ -246,37 +279,48 @@
 
     lax.fori_loop(0, T, inner_step, 0)
 
-    def second_copy(c, i):
+    @pl.when((half == 0) & ((z != 2) & (z != 1)))
+    def _():
+        pl.semaphore_wait(ready, 1)
+        send_far()
+
+    def second_copy(n, i):
+        cs = pl.ds(GROUPS[n][0], len(GROUPS[n]))
         return pltpu.make_async_remote_copy(
-            src_ref=s2.at[c, ring[i][0]], dst_ref=r2[c].at[pl.ds(me * SIDES, SIDES)], send_sem=ssem2.at[c],
-            recv_sem=rsem2.at[c], device_id=device(i, half), device_id_type=MESH)
+            src_ref=s2.at[ring[i][0], cs], dst_ref=r2[n].at[me], send_sem=ssem2.at[n], recv_sem=rsem2.at[n],
+            device_id=device(i, half), device_id_type=MESH)
+
+    def second_wait(n, sem):
+        part = r2[n].at[pl.ds(0, K - 1)]
+        pltpu.make_async_copy(part, part, sem.at[n]).wait()
 
     for copy in tables:
         copy.wait()
 
-    def collect(c):
-        all_rows(r1[c], rsem1.at[c], (2 * K - 1) * ROWS)
+    def collect(n):
+        for c in GROUPS[n]:
+            far_copy(n, c).wait_recv()
 
         def choose(k, carry):
             home = ((k // 4) * 8 + half * 4 + lax.rem(k, 4)) * T
             for r in range(SIDES):
-                s2[c, k, r] = r1[c][pick[r % 4, home + r // 4]]
+                at = pick[r % 4, home + r // 4]
+                for c in GROUPS[n]:
+                    s2[k, c, r] = r1[n][at >> 4, c - GROUPS[n][0], at & 15]
             return carry
 
         lax.fori_loop(0, K, choose, 0)
-
         for i in range(1, K):
-            second_copy(c, i).start()
-        r2[c][pl.ds(me * SIDES, SIDES)] = s2[c, me]
-
-    def finish(c):
-        all_rows(r2[c], rsem2.at[c], (K - 1) * SIDES)
-
+            second_copy(n, i).start()
+        for c in GROUPS[n]:
+            r2[n][me, c - GROUPS[n][0]] = s2[me, c]
+
+    def finish(n, c):
         def lay(t, carry):
             for s in range(4):
                 for d in range(2):
                     for a in range(C):
-                        halo[t * 4 + s, d, a:a + 1, :] = r2[c][place[d * 8 + a, s, tile * T + t] + 4 * t]
+                        halo[t * 4 + s, d, a:a + 1, :] = r2[n][place[d * 8 + a, s, tile * T + t], c - GROUPS[n][0], 4 * t + s]
             return carry
 
         lax.fori_loop(0, T, lay, 0)
@@ -295,15 +339,23 @@
 
         lax.fori_loop(0, T, add, 0)
 
-    for c in range(CH):
-        collect(c)
-        if c:
-            finish(c - 1)
-    finish(CH - 1)
-
-    for c in range(CH):
-        all_rows(r1[c], ssem1.at[c], (2 * K - 1) * ROWS)
-        all_rows(r2[c], ssem2.at[c], (K - 1) * SIDES)
+    def close(n):
+        second_wait(n, rsem2)
+        for c in GROUPS[n]:
+            finish(n, c)
+
+    for n in range(len(GROUPS)):
+        collect(n)
+        if n:
+            close(n - 1)
+    close(len(GROUPS) - 1)
+
+    for n in range(len(GROUPS)):
+        all_rows(r1[n], ssem1.at[n], K - 1)
+    for n, c in PARTS:
+        far_copy(n, c).wait_send()
+    for n in range(len(GROUPS)):
+        second_wait(n, ssem2)
     all_rows(flow, fcsend, Z)
     for n, way in enumerate((-1, 1)):
         for d in range(1, REACH + 1):
@@ -332,10 +384,10 @@
             pltpu.VMEM((T, C, 4, C), f32),
             *[pltpu.VMEM((4, 32 * T), jnp.int32)] * 2,
             dma((10,)),
-            pltpu.VMEM((CH, K, ROWS, 1, 128), f32),
-            *[pltpu.VMEM((2 * K * ROWS, 1, 128), f32)] * CH,
-            pltpu.VMEM((CH, K, SIDES, 1, 128), f32),
-            *[pltpu.VMEM((K * SIDES, 1, 128), f32)] * CH,
+            pltpu.VMEM((K, CH, ROWS, 1, 128), f32),
+            *[pltpu.VMEM((2 * K, len(g), ROWS, 1, 128), f32) for g in GROUPS],
+            pltpu.VMEM((K, CH, SIDES, 1, 128), f32),
+            *[pltpu.VMEM((K, len(g), SIDES, 1, 128), f32) for g in GROUPS],
             pltpu.VMEM((SIDES, 2, C, 128), f32),
             pltpu.VMEM((2 * Z, T, 4, FW), f32),
             pltpu.VMEM((128, FW), f32),
@@ -348,7 +400,7 @@
             pltpu.SMEM((4, 32 * T), jnp.int32),
             pltpu.SMEM((16, 4, 32 * T), jnp.int32),
             pltpu.SemaphoreType.REGULAR,
-            dma((CH,)), dma((CH,)), dma((CH,)), dma((CH,)),
+            *[dma((CH,))] * 6,
             dma((2, Z)), dma((2, Z)), dma, dma,
         ],
         compiler_params=pltpu.CompilerParams(collective_id=0, has_side_effects=True, vmem_limit_bytes=32 * 2**20),

time: 49.9 us -> 47.4 us (0.950)
  the two profiles are of different devices: /device:TPU:448 before, /device:TPU:257 now
where the time goes in v3:
time: 47.4 us; the launch traced here: 47.3 us
  Pallas kernels  46.6 us (98%)
  local copies, waits for them, and re-layouts  0.72 us (2%)
    pallas_call x1, Pallas kernels, shards(): pl.pallas_call(kernel, out_shape=pltpu.VMEM(tracers.shape, f32), in_specs...  46.6 us

profile of v3, /device:TPU:257, one launch (start us, length us, event | category | flops | bytes accessed | tf_op | source)
XLA Modules:
  0.0 47.3 jit_solution(9862155196474322797)
XLA Ops:
  0.0 46.6 %shard_map.82 = f32[3,8,8,384]{3,2,1,0:T(8,128)S(1)} custom-call(f32[3,8,8,384]{3,2,1,0:T(8,128)} %q_in.1, f32[3,8,4,9]{3,2,1,0:T(4,128)} %bitcast.7, f32[3,8,4,9]{3,2,1,0:T(4,128)} %bitcast.8, f32[3,8,4,9]{3,2,1,0:T(4,128)} %bitcast.9, f32[3,8,4,9]{3,2,1,0:T(4,128)} %bitcast.10, f32[3,8,4,8]{3,2,1,0:T(4,128)} %bitcast.11, s32[4,96]{1,0:T(4,128)} %bitcast.12, ...), custom_call_target="tpu_custom_call" | custom-call | tf_op jit(solution)/shard_map/pallas_call | solution.py:376
  46.6 0.7 %copy.10 = f32[3,8,8,384]{3,2,1,0:T(8,128)} copy(f32[3,8,8,384]{3,2,1,0:T(8,128)S(1)} %shard_map.82) | data formatting | bytes 589824

commit v4 on v3

--- a/solution.py
+++ b/solution.py
@@ -10,7 +10,7 @@
 C = 8
 GROUPS = ((0, 1), (2,))
 PARTS = tuple((n, c) for n, g in enumerate(GROUPS) for c in g)
-EARLY = 4
+EARLY = 5
 REACH = 4
 K = 16
 Z = 8
@@ -104,16 +104,15 @@
             src_ref=s1.at[ring[i][0], pl.ds(GROUPS[n][0], len(GROUPS[n]))], dst_ref=r1[n].at[me], send_sem=ssem1.at[n],
             recv_sem=rsem1.at[n], device_id=device(i, half), device_id_type=MESH)
 
-    def far_copy(n, c):
-        at = c - GROUPS[n][0]
+    def far_copy(n):
         return pltpu.make_async_remote_copy(
-            src_ref=r1[n].at[pl.ds(0, K), at], dst_ref=r1[n].at[pl.ds(K, K), at], send_sem=sfar.at[c],
-            recv_sem=rfar.at[c], device_id=device(0, 1 - half), device_id_type=MESH)
-
-    def early_copy(n, c, i):
+            src_ref=r1[n].at[pl.ds(0, K)], dst_ref=r1[n].at[pl.ds(K, K)], send_sem=sfar.at[n], recv_sem=rfar.at[n],
+            device_id=device(0, 1 - half), device_id_type=MESH)
+
+    def early_copy(n, i):
         return pltpu.make_async_remote_copy(
-            src_ref=s1.at[ring[i][0], c], dst_ref=r1[n].at[K + me, c - GROUPS[n][0]], send_sem=sfar.at[c], recv_sem=rfar.at[c],
-            device_id=device(i, 0), device_id_type=MESH)
+            src_ref=s1.at[ring[i][0], pl.ds(GROUPS[n][0], len(GROUPS[n]))], dst_ref=r1[n].at[K + me], send_sem=sfar.at[n],
+            recv_sem=rfar.at[n], device_id=device(i, 0), device_id_type=MESH)
 
     def send_far():
         for n in range(len(GROUPS)):
@@ -121,8 +120,8 @@
 
         @pl.when((half == 0) | jnp.logical_not(early))
         def _():
-            for n, c in PARTS:
-                far_copy(n, c).start()
+            for n in range(len(GROUPS)):
+                far_copy(n).start()
 
     def block(zz):
         return flow.at[zz * 2 + core]
@@ -157,9 +156,9 @@
 
         @pl.when(early)
         def _():
-            for n, c in PARTS:
+            for n in range(len(GROUPS)):
                 for i in range(K):
-                    early_copy(n, c, i).start()
+                    early_copy(n, i).start()
 
     def pack(t, carry):
         flow[tag, t] = jnp.zeros((4, FW), jnp.float32)
@@ -298,8 +297,7 @@
         copy.wait()
 
     def collect(n):
-        for c in GROUPS[n]:
-            far_copy(n, c).wait_recv()
+        far_copy(n).wait_recv()
 
         def choose(k, carry):
             home = ((k // 4) * 8 + half * 4 + lax.rem(k, 4)) * T
@@ -352,8 +350,7 @@
 
     for n in range(len(GROUPS)):
         all_rows(r1[n], ssem1.at[n], K - 1)
-    for n, c in PARTS:
-        far_copy(n, c).wait_send()
+        far_copy(n).wait_send()
     for n in range(len(GROUPS)):
         second_wait(n, ssem2)
     all_rows(flow, fcsend, Z)

time: 47.4 us -> 46.5 us (0.981)
  the two profiles are of different devices: /device:TPU:257 before, /device:TPU:128 now
where the time goes in v4:
time: 46.5 us; the launch traced here: 46.4 us
  Pallas kernels  45.7 us (98%)
  local copies, waits for them, and re-layouts  0.72 us (2%)
    pallas_call x1, Pallas kernels, shards(): pl.pallas_call(kernel, out_shape=pltpu.VMEM(tracers.shape, f32), in_specs...  45.7 us

profile of v4, /device:TPU:128, one launch (start us, length us, event | category | flops | bytes accessed | tf_op | source)
XLA Modules:
  0.0 46.4 jit_solution(3571222957646768336)
XLA Ops:
  0.0 45.7 %shard_map.82 = f32[3,8,8,384]{3,2,1,0:T(8,128)S(1)} custom-call(f32[3,8,8,384]{3,2,1,0:T(8,128)} %q_in.1, f32[3,8,4,9]{3,2,1,0:T(4,128)} %bitcast.7, f32[3,8,4,9]{3,2,1,0:T(4,128)} %bitcast.8, f32[3,8,4,9]{3,2,1,0:T(4,128)} %bitcast.9, f32[3,8,4,9]{3,2,1,0:T(4,128)} %bitcast.10, f32[3,8,4,8]{3,2,1,0:T(4,128)} %bitcast.11, s32[4,96]{1,0:T(4,128)} %bitcast.12, ...), custom_call_target="tpu_custom_call" | custom-call | tf_op jit(solution)/shard_map/pallas_call | solution.py:373
  45.7 0.7 %copy.10 = f32[3,8,8,384]{3,2,1,0:T(8,128)} copy(f32[3,8,8,384]{3,2,1,0:T(8,128)S(1)} %shard_map.82) | data formatting | bytes 589824

commit v5 on v4

--- a/solution.py
+++ b/solution.py
@@ -13,6 +13,7 @@
 EARLY = 5
 REACH = 4
 K = 16
+FAR_FIRST = sorted(range(1, K), key=lambda i: -min(i // 4, 4 - i // 4) - min(i % 4, 4 - i % 4))
 Z = 8
 CH = 3
 ROWS = 9
@@ -140,7 +141,7 @@
 
     def plane_out():
         for n in range(len(GROUPS)):
-            for i in range(1, K):
+            for i in FAR_FIRST:
                 first_copy(n, i).start()
         for n, c in PARTS:
             r1[n][me, c - GROUPS[n][0]] = s1[me, c]
@@ -308,7 +309,7 @@
             return carry
 
         lax.fori_loop(0, K, choose, 0)
-        for i in range(1, K):
+        for i in FAR_FIRST:
             second_copy(n, i).start()
         for c in GROUPS[n]:
             r2[n][me, c - GROUPS[n][0]] = s2[me, c]

time: 46.5 us -> 46.5 us (level)
  no operation moved by 1% of the time
where the time goes in v5:
time: 46.5 us; the launch traced here: 46.3 us
  Pallas kernels  45.6 us (98%)
  local copies, waits for them, and re-layouts  0.72 us (2%)
    pallas_call x1, Pallas kernels, shards(): pl.pallas_call(kernel, out_shape=pltpu.VMEM(tracers.shape, f32), in_specs...  45.6 us

profile of v5, /device:TPU:128, one launch (start us, length us, event | category | flops | bytes accessed | tf_op | source)
XLA Modules:
  0.0 46.3 jit_solution(4073170731262086953)
XLA Ops:
  0.0 45.6 %shard_map.82 = f32[3,8,8,384]{3,2,1,0:T(8,128)S(1)} custom-call(f32[3,8,8,384]{3,2,1,0:T(8,128)} %q_in.1, f32[3,8,4,9]{3,2,1,0:T(4,128)} %bitcast.7, f32[3,8,4,9]{3,2,1,0:T(4,128)} %bitcast.8, f32[3,8,4,9]{3,2,1,0:T(4,128)} %bitcast.9, f32[3,8,4,9]{3,2,1,0:T(4,128)} %bitcast.10, f32[3,8,4,8]{3,2,1,0:T(4,128)} %bitcast.11, s32[4,96]{1,0:T(4,128)} %bitcast.12, ...), custom_call_target="tpu_custom_call" | custom-call | tf_op jit(solution)/shard_map/pallas_call | solution.py:374
  45.6 0.7 %copy.10 = f32[3,8,8,384]{3,2,1,0:T(8,128)} copy(f32[3,8,8,384]{3,2,1,0:T(8,128)S(1)} %shard_map.82) | data formatting | bytes 589824
